TPU v7x, 32 devices: a whole 2x2x4 slice. The times are simulated.
32 devices in a mesh: clips: 2 (over y), tile: 4 (over x, core), tm: 4 (over z).
Axes of the slice: x: 2, y: 2, z: 4, core: 2. Of those that a mesh axis runs over, the one named last changes fastest.
Arguments:
- frames: bfloat16 [8, 120, 32, 128], P(('clips', 'tm'), None, 'tile'), parts along dimension 0, may hold values from -6 to 6
- ln_gain: float32 [2, 2, 120], replicated, may hold values from 0.5 to 1.5
- qkv_weight: bfloat16 [2, 120, 360], replicated, may hold values from -4 to 4
- out_weight: bfloat16 [2, 120, 120], replicated, may hold values from -0.5 to 0.5
- gate_weight: bfloat16 [2, 120, 240], replicated, may hold values from -0.5 to 0.5
- up_weight: bfloat16 [2, 120, 240], replicated, may hold values from -0.5 to 0.5
- down_weight: bfloat16 [2, 240, 120], replicated, may hold values from -0.375 to 0.375
- conv_weight: bfloat16 [2, 9, 120, 120], replicated, may hold values from -0.1875 to 0.1875
- conv_bias: float32 [2, 120], replicated, may hold values from -3 to 3
Outputs:
- restored: bfloat16 [8, 120, 32, 128], P(('clips', 'tm'), None, 'tile'), parts along dimension 0
There are 2 independent parts, one for each index of `clips`. A program takes and returns all parts, laid end to end along the dimension named above; an argument that names none is the same for every part. Nothing has to cross between parts.
All inputs are finite; a program needn't handle non-finite values.
Results may differ from a plain program's by a relative error of at most 0.0084.
Values may be sent and summed in bfloat16 or wider, within the bound.
A program may use at most 64 MiB of HBM per device.

v0:
```python
import functools

import jax
import jax.numpy as jnp
from jax import lax
from jax.experimental import pallas as pl
from jax.experimental.pallas import tpu as pltpu
from jax.sharding import PartitionSpec as P

HEADS = 6
HD = 20
LAYERS = 2
LANES = 128
WIN = 8
HALF = WIN // 2
GROUP = 4
F32 = jnp.float32
BF16 = jnp.bfloat16
MESH = pl.DeviceIdType.MESH


def dot(a, b):
    return lax.dot_general(a, b, (((1,), (0,)), ((), ())), preferred_element_type=F32)


def dot_nt(a, b):
    return lax.dot_general(a, b, (((1,), (1,)), ((), ())), preferred_element_type=F32)


def lanes_of(shape):
    return lax.broadcasted_iota(jnp.int32, shape, len(shape) - 1)


def layer_norm(x, gain, channels):
    mean = jnp.sum(x, axis=-1, keepdims=True) * (1.0 / channels)
    center = jnp.where(lanes_of(x.shape) < channels, x - mean, 0.0)
    spread = jnp.sum(center * center, axis=-1, keepdims=True) * (1.0 / channels)
    return center * lax.rsqrt(spread + 1e-05) * gain


def kernel(
    frames, ln_gain, qkv_w, out_w, gate_w, up_w, down_w, conv_w, conv_b, out,
    xs, stream, kv0, kv1, bsend, ret, mix0, mix1, yp0, yp1,
    pq, po, pgu, pd, pc, tmp, small,
    send0, recv0, send1, recv1, send_ret, recv_ret, send_halo, recv_halo,
):
    channels, rows, cols = frames.shape[1:]
    hidden = gate_w.shape[2]
    windows = cols // WIN
    groups = windows // GROUP
    tiles, count = lax.axis_size("tile"), lax.axis_size("tm")
    t, f = lax.axis_index("tile"), lax.axis_index("tm")
    odd = lax.rem(f, 2)
    even_pair = f + 1 - 2 * odd
    odd_pair = lax.rem(f + 2 * odd - 1 + count, count)
    above, below = lax.rem(t + tiles - 1, tiles), lax.rem(t + 1, tiles)

    barrier = pltpu.get_barrier_semaphore()
    peers = [
        {"tm": even_pair}, {"tm": odd_pair}, {"tile": above}, {"tile": below},
        {"tile": above, "tm": odd_pair}, {"tile": below, "tm": odd_pair},
    ]
    for peer in peers:
        pl.semaphore_signal(barrier, inc=1, device_id=peer, device_id_type=MESH)

    def remote(src, dst, send, recv, peer):
        return pltpu.make_async_remote_copy(
            src_ref=src, dst_ref=dst, send_sem=send, recv_sem=recv,
            device_id=peer, device_id_type=MESH,
        )

    def pair_copy(g):
        at = pl.ds(g * GROUP, GROUP)
        return remote(
            kv0.at[at, pl.ds(0, 64)], kv0.at[at, pl.ds(64, 64)],
            send0.at[g], recv0.at[g], {"tm": even_pair},
        )

    def odd_copies(g):
        at = pl.ds(g * GROUP, GROUP)
        return [
            remote(kv1.at[at, pl.ds(0, 32)], kv1.at[at, pl.ds(64, 32)],
                   send1.at[0, g], recv1.at[0, g], {"tm": odd_pair}),
            remote(bsend.at[at], kv1.at[at, pl.ds(96, 32)],
                   send1.at[1, g], recv1.at[1, g], {"tile": above, "tm": odd_pair}),
            remote(bsend.at[at], kv1.at[at, pl.ds(32, 32)],
                   send1.at[2, g], recv1.at[2, g], {"tile": above}),
        ]

    def ret_copy(g):
        at = pl.ds(g * GROUP, GROUP)
        return remote(ret.at[at], mix1.at[0, at], send_ret.at[g], recv_ret.at[g], {"tile": below})

    def halo_copy(layer, side):
        yp = (yp0, yp1)[layer]
        if side == 0:
            src, dst, peer = yp.at[1], yp.at[rows + 1], {"tile": above}
        else:
            src, dst, peer = yp.at[rows], yp.at[0], {"tile": below}
        return remote(src, dst, send_halo.at[layer, side], recv_halo.at[layer, side], peer)

    small[...] = jnp.zeros_like(small)
    for layer in range(LAYERS):
        small[2 * layer : 2 * layer + 2, 0:channels] = ln_gain[layer]
    small[4 : 4 + LAYERS, 0:channels] = conv_b[...]

    xs[...] = frames[0].astype(F32).reshape(channels * rows, cols)
    for r in range(rows):
        row = xs[pl.ds(r, channels, stride=rows), :]
        row = jnp.concatenate([row, jnp.zeros((LANES - channels, cols), F32)], axis=0)
        stream[r // HALF, :, r % HALF] = row.T.reshape(windows, WIN, LANES)

    for g in range(groups):
        at = pl.ds(g * GROUP, GROUP)
        for half in range(2):
            x = stream[half, at].reshape(GROUP * 32, LANES)
            normed = layer_norm(x, small[0:1, :], channels)
            kv0[at, pl.ds(32 * half, 32)] = normed.astype(BF16).reshape(GROUP, 32, LANES)
        if g == 0:
            pl.semaphore_wait(barrier, len(peers))
        pair_copy(g).start()

    tmp[...] = jnp.zeros_like(tmp)
    for layer in range(LAYERS):
        tmp[0:channels, 0 : 3 * channels] = qkv_w[layer].astype(F32)
        whole = tmp[0:LANES, 0:384]
        for j in range(3):
            part = whole if j == 0 else pltpu.roll(whole, 384 - channels * j, 1)
            part = part[:, 0:LANES]
            part = jnp.where(lanes_of(part.shape) < channels, part, 0.0)
            pq[layer, :, LANES * j : LANES * (j + 1)] = part.astype(BF16)
        tmp[0:LANES, 0:384] = jnp.zeros((LANES, 384), F32)
        for j, weight in enumerate((gate_w, up_w)):
            tmp[0:channels, 0:hidden] = weight[layer].astype(F32)
            pgu[layer, :, 256 * j : 256 * (j + 1)] = tmp[0:LANES, 0:256].astype(BF16)
        tmp[0:LANES, 0:256] = jnp.zeros((LANES, 256), F32)
        tmp[0:channels, 0:channels] = out_w[layer].astype(F32)
        po[layer] = tmp[0:LANES, 0:LANES].astype(BF16)
        for a in range(3):
            for b in range(3):
                tmp[0:channels, 0:channels] = conv_w[layer, 3 * a + b].astype(F32)
                pc[layer, LANES * a : LANES * (a + 1), LANES * b : LANES * (b + 1)] = tmp[
                    0:LANES, 0:LANES
                ].astype(BF16)
        tmp[0:hidden, 0:channels] = down_w[layer].astype(F32)
        pd[layer] = tmp[0:256, 0:LANES].astype(BF16)
        tmp[0:256, 0:LANES] = jnp.zeros((256, LANES), F32)

    scale = HD ** (-0.5) * 1.4426950408889634

    def attend(layer, kv, g, put):
        at = pl.ds(g * GROUP, GROUP)
        all_in = kv[at].reshape(GROUP * 128, LANES)
        q_in = kv[at, pl.ds(0, 64)].reshape(GROUP * 64, LANES)
        packed = dot(all_in, pq[layer, :, LANES:384]).astype(BF16)
        queries = dot(q_in, pq[layer, :, 0:LANES]).astype(BF16).astype(F32)
        lane = lanes_of((64, LANES))
        head = [(lane >= HD * h) & (lane < HD * (h + 1)) for h in range(HEADS)]
        ones = jnp.ones((128, LANES), BF16)
        for i in range(GROUP):
            q = queries[64 * i : 64 * (i + 1)]
            q = jnp.concatenate([jnp.where(head[h], q, 0.0).astype(BF16) for h in range(HEADS)], axis=0)
            k = packed[128 * i : 128 * (i + 1), 0:LANES]
            v = jnp.concatenate([packed[128 * i : 128 * (i + 1), LANES:256], ones], axis=1)
            scores = dot_nt(q, k)
            top = jnp.max(scores, axis=-1, keepdims=True)
            weights = jnp.exp2((scores - top) * scale).astype(BF16)
            both = dot(weights, v)
            mixed, total = both[0:64, 0:LANES], both[0:64, LANES:256]
            for h in range(1, HEADS):
                mixed = jnp.where(head[h], both[64 * h : 64 * (h + 1), 0:LANES], mixed)
                total = jnp.where(head[h], both[64 * h : 64 * (h + 1), LANES:256], total)
            mixed = (mixed / total).astype(BF16)
            put(g * GROUP + i, mixed)

    def feed(layer, mix, half):
        piece = 8
        yp = (yp0, yp1)[layer]
        for p in range(windows // piece):
            at = pl.ds(piece * p, piece)
            x = stream[half, at].reshape(piece * 32, LANES)
            x = x + dot(mix[half, at].reshape(piece * 32, LANES), po[layer])
            normed = layer_norm(x, small[2 * layer + 1 : 2 * layer + 2, :], channels).astype(BF16)
            gate = dot(normed, pgu[layer, :, 0:256])
            up = dot(normed, pgu[layer, :, 256:512])
            act = 0.5 * gate * (1.0 + lax.erf(gate * 0.7071067811865476)) * up
            x = x + dot(act.astype(BF16), pd[layer])
            stream[half, at] = x.reshape(piece, HALF, WIN, LANES)
        for i in range(HALF):
            yp[1 + HALF * half + i] = stream[half, :, i].reshape(cols, LANES).astype(BF16)

    def convolve(layer, r, first_col, last_col):
        yp = (yp0, yp1)[layer]
        parts = [yp[r], yp[r + 1], yp[r + 2]]
        if r == 0:
            parts[0] = jnp.where(t == 0, jnp.zeros_like(parts[0]), parts[0])
        if r == rows - 1:
            parts[2] = jnp.where(t == tiles - 1, jnp.zeros_like(parts[2]), parts[2])
        taps = dot(jnp.concatenate(parts, axis=1), pc[layer])
        at = lax.broadcasted_iota(jnp.int32, (cols, LANES), 0)
        total = taps[:, LANES : 2 * LANES]
        total += jnp.where(at == first_col, 0.0, pltpu.roll(taps[:, 0:LANES], 1, 0))
        total += jnp.where(at == last_col, 0.0, pltpu.roll(taps[:, 2 * LANES :], cols - 1, 0))
        fed = stream[r // HALF, :, r % HALF].reshape(cols, LANES)
        return fed + (total + small[4 + layer : 5 + layer, :])

    inner = list(range(1, rows - 1))

    def put0(n, mixed):
        mix0[0, n] = mixed[0:32]
        mix0[1, n] = mixed[32:64]

    def step0(g, carry):
        pair_copy(g).wait_recv()
        attend(0, kv0, g, put0)
        return carry

    lax.fori_loop(0, groups, step0, 0)
    for half in range(2):
        feed(0, mix0, half)
        halo_copy(0, half).start()

    def finish0(r):
        row = pltpu.roll(convolve(0, r, 0, cols - 1), cols - HALF, 0)
        stream[r // HALF, :, r % HALF] = row.reshape(windows, WIN, LANES)

    for r in inner:
        finish0(r)
    for side in range(2):
        halo_copy(0, side).wait_recv()
    finish0(0)
    finish0(rows - 1)

    for g in range(groups):
        at = pl.ds(g * GROUP, GROUP)
        for half in range(2):
            x = stream[half, at].reshape(GROUP * 32, LANES)
            normed = layer_norm(x, small[2:3, :], channels).astype(BF16).reshape(GROUP, 32, LANES)
            if half == 0:
                bsend[at] = normed
            else:
                kv1[at, pl.ds(0, 32)] = normed
        for copy in odd_copies(g):
            copy.start()

    def put1(n, mixed):
        mix1[1, n] = mixed[0:32]
        ret[n] = mixed[32:64]

    def step1(g, carry):
        for copy in odd_copies(g):
            copy.wait_recv()
        attend(1, kv1, g, put1)
        ret_copy(g).start()
        return carry

    lax.fori_loop(0, groups, step1, 0)
    feed(1, mix1, 1)
    halo_copy(1, 1).start()
    for g in range(groups):
        ret_copy(g).wait_recv()
    feed(1, mix1, 0)
    halo_copy(1, 0).start()

    def finish1(r):
        row = convolve(1, r, cols - HALF, cols - HALF - 1)
        row = pltpu.roll(row.T, HALF, 1)
        xs[pl.ds(r, channels, stride=rows), :] = row[0:channels]

    for r in inner:
        finish1(r)
    for side in range(2):
        halo_copy(1, side).wait_recv()
    finish1(0)
    finish1(rows - 1)
    out[0] = xs[...].reshape(channels, rows, cols).astype(BF16)

    for g in range(groups):
        pair_copy(g).wait_send()
        for copy in odd_copies(g):
            copy.wait_send()
        ret_copy(g).wait_send()
    for layer in range(LAYERS):
        for side in range(2):
            halo_copy(layer, side).wait_send()


def on_device(*args):
    frames = args[0]
    _, channels, rows, cols = frames.shape
    windows = cols // WIN
    groups = windows // GROUP
    dma = pltpu.SemaphoreType.DMA
    vmem = pl.BlockSpec(memory_space=pltpu.VMEM)
    return pl.pallas_call(
        kernel,
        out_shape=jax.ShapeDtypeStruct(frames.shape, BF16),
        in_specs=[vmem] * len(args),
        out_specs=vmem,
        scratch_shapes=[
            pltpu.VMEM((channels * rows, cols), F32),
            pltpu.VMEM((2, windows, HALF, WIN, LANES), F32),
            pltpu.VMEM((windows, 128, LANES), BF16),
            pltpu.VMEM((windows, 128, LANES), BF16),
            pltpu.VMEM((windows, 32, LANES), BF16),
            pltpu.VMEM((windows, 32, LANES), BF16),
            pltpu.VMEM((2, windows, 32, LANES), BF16),
            pltpu.VMEM((2, windows, 32, LANES), BF16),
            pltpu.VMEM((rows + 2, cols, LANES), BF16),
            pltpu.VMEM((rows + 2, cols, LANES), BF16),
            pltpu.VMEM((LAYERS, LANES, 384), BF16),
            pltpu.VMEM((LAYERS, LANES, LANES), BF16),
            pltpu.VMEM((LAYERS, LANES, 512), BF16),
            pltpu.VMEM((LAYERS, 256, LANES), BF16),
            pltpu.VMEM((LAYERS, 384, 384), BF16),
            pltpu.VMEM((256, 384), F32),
            pltpu.VMEM((8, LANES), F32),
            dma((groups,)), dma((groups,)),
            dma((3, groups)), dma((3, groups)),
            dma((groups,)), dma((groups,)),
            dma((LAYERS, 2)), dma((LAYERS, 2)),
        ],
        compiler_params=pltpu.CompilerParams(
            collective_id=0, has_side_effects=True, vmem_limit_bytes=40 * 2**20
        ),
    )(*args)


def solution(mesh):
    in_specs = (P(("clips", "tm"), None, "tile", None), P(), P(), P(), P(), P(), P(), P(), P())
    out_specs = P(("clips", "tm"), None, "tile", None)
    return jax.shard_map(
        on_device, mesh=mesh, in_specs=in_specs, out_specs=out_specs, check_vma=False
    )
```

profile of v0, /device:TPU:13, one launch (start us, length us, event | category | flops | bytes accessed | tf_op | source)
XLA Modules:
  0.0 45.6 jit_solution(16918944553327547455)
XLA Ops:
  0.0 0.0 copy-start
  0.0 1.0 %copy-done = bf16[2,9,120,120]{3,2,1,0:T(8,128)(2,1)S(1)} copy-done((bf16[2,9,120,120]{3,2,1,0:T(8,128)(2,1)S(1)}, bf16[2,9,120,120]{3,2,1,0:T(8,128)(2,1)}, u32[]{:S(2)}) %copy-start) | copy-done | bytes 518424
  1.1 0.0 copy-start.1
  1.1 0.9 %copy-done.1 = bf16[1,120,8,128]{3,2,1,0:T(8,128)(2,1)S(1)} copy-done((bf16[1,120,8,128]{3,2,1,0:T(8,128)(2,1)S(1)}, bf16[1,120,8,128]{3,2,1,0:T(8,128)(2,1)}, u32[]{:S(2)}) %copy-start.1) | copy-done | bytes 245784
  2.0 0.0 copy-start.2
  2.0 0.9 %copy-done.2 = bf16[2,120,360]{2,1,0:T(8,128)(2,1)S(1)} copy-done((bf16[2,120,360]{2,1,0:T(8,128)(2,1)S(1)}, bf16[2,120,360]{2,1,0:T(8,128)(2,1)}, u32[]{:S(2)}) %copy-start.2) | copy-done | bytes 172824
  2.9 0.0 copy-start.3
  2.9 0.9 %copy-done.3 = bf16[2,120,240]{2,1,0:T(8,128)(2,1)S(1)} copy-done((bf16[2,120,240]{2,1,0:T(8,128)(2,1)S(1)}, bf16[2,120,240]{2,1,0:T(8,128)(2,1)}, u32[]{:S(2)}) %copy-start.3) | copy-done | bytes 115224
  3.8 0.0 copy-start.4
  3.8 0.9 %copy-done.4 = bf16[2,120,240]{2,1,0:T(8,128)(2,1)S(1)} copy-done((bf16[2,120,240]{2,1,0:T(8,128)(2,1)S(1)}, bf16[2,120,240]{2,1,0:T(8,128)(2,1)}, u32[]{:S(2)}) %copy-start.4) | copy-done | bytes 115224
  4.7 0.0 copy-start.5
  4.7 0.9 %copy-done.5 = bf16[2,240,120]{2,1,0:T(8,128)(2,1)S(1)} copy-done((bf16[2,240,120]{2,1,0:T(8,128)(2,1)S(1)}, bf16[2,240,120]{2,1,0:T(8,128)(2,1)}, u32[]{:S(2)}) %copy-start.5) | copy-done | bytes 115224
  5.6 0.0 copy-start.6
  5.6 0.8 %copy-done.6 = bf16[2,120,120]{2,1,0:T(8,128)(2,1)S(1)} copy-done((bf16[2,120,120]{2,1,0:T(8,128)(2,1)S(1)}, bf16[2,120,120]{2,1,0:T(8,128)(2,1)}, u32[]{:S(2)}) %copy-start.6) | copy-done | bytes 57624
  6.5 0.0 copy-start.7
  6.5 0.7 %copy-done.7 = f32[2,2,120]{2,1,0:T(2,128)S(1)} copy-done((f32[2,2,120]{2,1,0:T(2,128)S(1)}, f32[2,2,120]{2,1,0:T(2,128)}, u32[]{:S(2)}) %copy-start.7) | copy-done | bytes 1944
  7.1 0.0 copy-start.8
  7.1 0.7 %copy-done.8 = f32[2,120]{1,0:T(2,128)S(1)} copy-done((f32[2,120]{1,0:T(2,128)S(1)}, f32[2,120]{1,0:T(2,128)}, u32[]{:S(2)}) %copy-start.8) | copy-done | bytes 984
  7.8 37.0 %shard_map.91 = bf16[1,120,8,128]{3,2,1,0:T(8,128)(2,1)S(1)} custom-call(bf16[1,120,8,128]{3,2,1,0:T(8,128)(2,1)S(1)} %copy-done.1, f32[2,2,120]{2,1,0:T(2,128)S(1)} %copy-done.7, bf16[2,120,360]{2,1,0:T(8,128)(2,1)S(1)} %copy-done.2, bf16[2,120,120]{2,1,0:T(8,128)(2,1)S(1)} %copy-done.6, bf16[2,120,240]{2,1,0:T(8,128)(2,1)S(1)} %copy-done.3, ...), custom_call_target="tpu_custom_call" | custom-call | tf_op jit(solution)/shard_map/pallas_call | solution.py:295
  44.9 0.7 %copy.11 = bf16[1,120,8,128]{3,2,1,0:T(8,128)(2,1)} copy(bf16[1,120,8,128]{3,2,1,0:T(8,128)(2,1)S(1)} %shard_map.91) | data formatting | bytes 491520
Async XLA Ops:
  0.0 1.1 %copy-start = (bf16[2,9,120,120]{3,2,1,0:T(8,128)(2,1)S(1)}, bf16[2,9,120,120]{3,2,1,0:T(8,128)(2,1)}, u32[]{:S(2)}) copy-start(bf16[2,9,120,120]{3,2,1,0:T(8,128)(2,1)} %conv_w.1) | copy-start | bytes 1555204
  1.1 0.9 %copy-start.1 = (bf16[1,120,8,128]{3,2,1,0:T(8,128)(2,1)S(1)}, bf16[1,120,8,128]{3,2,1,0:T(8,128)(2,1)}, u32[]{:S(2)}) copy-start(bf16[1,120,8,128]{3,2,1,0:T(8,128)(2,1)} %frames.1) | copy-start | bytes 737284
  2.0 0.9 %copy-start.2 = (bf16[2,120,360]{2,1,0:T(8,128)(2,1)S(1)}, bf16[2,120,360]{2,1,0:T(8,128)(2,1)}, u32[]{:S(2)}) copy-start(bf16[2,120,360]{2,1,0:T(8,128)(2,1)} %qkv_w.1) | copy-start | bytes 518404
  2.9 0.9 %copy-start.3 = (bf16[2,120,240]{2,1,0:T(8,128)(2,1)S(1)}, bf16[2,120,240]{2,1,0:T(8,128)(2,1)}, u32[]{:S(2)}) copy-start(bf16[2,120,240]{2,1,0:T(8,128)(2,1)} %gate_w.1) | copy-start | bytes 345604
  3.8 0.9 %copy-start.4 = (bf16[2,120,240]{2,1,0:T(8,128)(2,1)S(1)}, bf16[2,120,240]{2,1,0:T(8,128)(2,1)}, u32[]{:S(2)}) copy-start(bf16[2,120,240]{2,1,0:T(8,128)(2,1)} %up_w.1) | copy-start | bytes 345604
  4.7 0.9 %copy-start.5 = (bf16[2,240,120]{2,1,0:T(8,128)(2,1)S(1)}, bf16[2,240,120]{2,1,0:T(8,128)(2,1)}, u32[]{:S(2)}) copy-start(bf16[2,240,120]{2,1,0:T(8,128)(2,1)} %down_w.1) | copy-start | bytes 345604
  5.6 0.8 %copy-start.6 = (bf16[2,120,120]{2,1,0:T(8,128)(2,1)S(1)}, bf16[2,120,120]{2,1,0:T(8,128)(2,1)}, u32[]{:S(2)}) copy-start(bf16[2,120,120]{2,1,0:T(8,128)(2,1)} %out_w.1) | copy-start | bytes 172804
  6.5 0.7 %copy-start.7 = (f32[2,2,120]{2,1,0:T(2,128)S(1)}, f32[2,2,120]{2,1,0:T(2,128)}, u32[]{:S(2)}) copy-start(f32[2,2,120]{2,1,0:T(2,128)} %ln_gain.1) | copy-start | bytes 5764
  7.1 0.7 %copy-start.8 = (f32[2,120]{1,0:T(2,128)S(1)}, f32[2,120]{1,0:T(2,128)}, u32[]{:S(2)}) copy-start(f32[2,120]{1,0:T(2,128)} %conv_b.1) | copy-start | bytes 2884
where the time goes:
time: 45.9 us; the launch traced here: 45.6 us
  Pallas kernels  37 us (81%)
  local copies, waits for them, and re-layouts  8.5 us (19%)
    pallas_call x1, Pallas kernels, on_device(): pl.pallas_call(kernel, out_shape=jax.ShapeDtypeStruct(frames.shape, BF16)...  37 us
    unnamed x19, local copies, waits for them, and re-layouts  8.5 us

commit v1 on v0

--- a/solution.py
+++ b/solution.py
@@ -39,8 +39,9 @@
 
 
 def kernel(
-    frames, ln_gain, qkv_w, out_w, gate_w, up_w, down_w, conv_w, conv_b, out,
-    xs, stream, kv0, kv1, bsend, ret, mix0, mix1, yp0, yp1,
+    frames_h, ln_gain_h, qkv_h, out_h, gate_h, up_h, down_h, conv_h, conv_b_h, out,
+    frames, ln_gain, qkv_w, out_w, gate_w, up_w, down_w, conv_w, conv_b, load_sem,
+    xs, stream, fedn, taps, kv0, kv1, bsend, ret, mix0, mix1, yp0, yp1,
     pq, po, pgu, pd, pc, tmp, small,
     send0, recv0, send1, recv1, send_ret, recv_ret, send_halo, recv_halo,
 ):
@@ -48,6 +49,7 @@
     hidden = gate_w.shape[2]
     windows = cols // WIN
     groups = windows // GROUP
+    span = GROUP * WIN
     tiles, count = lax.axis_size("tile"), lax.axis_size("tm")
     t, f = lax.axis_index("tile"), lax.axis_index("tm")
     odd = lax.rem(f, 2)
@@ -55,6 +57,13 @@
     odd_pair = lax.rem(f + 2 * odd - 1 + count, count)
     above, below = lax.rem(t + tiles - 1, tiles), lax.rem(t + 1, tiles)
 
+    pairs = [
+        (frames_h, frames), (ln_gain_h, ln_gain), (conv_b_h, conv_b), (qkv_h, qkv_w), (out_h, out_w),
+        (gate_h, gate_w), (up_h, up_w), (down_h, down_w), (conv_h, conv_w),
+    ]
+    loads = [pltpu.make_async_copy(a, b, load_sem.at[i]) for i, (a, b) in enumerate(pairs)]
+    for load in loads:
+        load.start()
     barrier = pltpu.get_barrier_semaphore()
     peers = [
         {"tm": even_pair}, {"tm": odd_pair}, {"tile": above}, {"tile": below},
@@ -91,14 +100,18 @@
         at = pl.ds(g * GROUP, GROUP)
         return remote(ret.at[at], mix1.at[0, at], send_ret.at[g], recv_ret.at[g], {"tile": below})
 
-    def halo_copy(layer, side):
+    def halo_copy(layer, side, g=0):
         yp = (yp0, yp1)[layer]
+        at = pl.ds(g * span, span) if layer == 0 else pl.ds(0, cols)
+        slot = g if layer == 0 else groups
         if side == 0:
-            src, dst, peer = yp.at[1], yp.at[rows + 1], {"tile": above}
+            src, dst, peer = yp.at[1, at], yp.at[rows + 1, at], {"tile": above}
         else:
-            src, dst, peer = yp.at[rows], yp.at[0], {"tile": below}
-        return remote(src, dst, send_halo.at[layer, side], recv_halo.at[layer, side], peer)
-
+            src, dst, peer = yp.at[rows, at], yp.at[0, at], {"tile": below}
+        return remote(src, dst, send_halo.at[slot, side], recv_halo.at[slot, side], peer)
+
+    for load in loads[0:3]:
+        load.wait()
     small[...] = jnp.zeros_like(small)
     for layer in range(LAYERS):
         small[2 * layer : 2 * layer + 2, 0:channels] = ln_gain[layer]
@@ -120,8 +133,11 @@
             pl.semaphore_wait(barrier, len(peers))
         pair_copy(g).start()
 
+    for load in loads[3:]:
+        load.wait()
     tmp[...] = jnp.zeros_like(tmp)
-    for layer in range(LAYERS):
+
+    def pad_weights(layer):
         tmp[0:channels, 0 : 3 * channels] = qkv_w[layer].astype(F32)
         whole = tmp[0:LANES, 0:384]
         for j in range(3):
@@ -146,6 +162,8 @@
         pd[layer] = tmp[0:256, 0:LANES].astype(BF16)
         tmp[0:256, 0:LANES] = jnp.zeros((256, LANES), F32)
 
+    pad_weights(0)
+
     scale = HD ** (-0.5) * 1.4426950408889634
 
     def attend(layer, kv, g, put):
@@ -173,21 +191,46 @@
             mixed = (mixed / total).astype(BF16)
             put(g * GROUP + i, mixed)
 
-    def feed(layer, mix, half):
-        piece = 8
-        yp = (yp0, yp1)[layer]
-        for p in range(windows // piece):
-            at = pl.ds(piece * p, piece)
-            x = stream[half, at].reshape(piece * 32, LANES)
-            x = x + dot(mix[half, at].reshape(piece * 32, LANES), po[layer])
-            normed = layer_norm(x, small[2 * layer + 1 : 2 * layer + 2, :], channels).astype(BF16)
-            gate = dot(normed, pgu[layer, :, 0:256])
-            up = dot(normed, pgu[layer, :, 256:512])
-            act = 0.5 * gate * (1.0 + lax.erf(gate * 0.7071067811865476)) * up
-            x = x + dot(act.astype(BF16), pd[layer])
-            stream[half, at] = x.reshape(piece, HALF, WIN, LANES)
+    def feed(layer, mix, half, g):
+        at = pl.ds(g * GROUP, GROUP)
+        x = stream[half, at].reshape(GROUP * 32, LANES)
+        x = x + dot(mix[half, at].reshape(GROUP * 32, LANES), po[layer])
+        normed = layer_norm(x, small[2 * layer + 1 : 2 * layer + 2, :], channels).astype(BF16)
+        gate = dot(normed, pgu[layer, :, 0:256])
+        up = dot(normed, pgu[layer, :, 256:512])
+        act = 0.5 * gate * (1.0 + lax.erf(gate * 0.7071067811865476)) * up
+        x = x + dot(act.astype(BF16), pd[layer])
+        stream[half, at] = x.reshape(GROUP, HALF, WIN, LANES)
         for i in range(HALF):
-            yp[1 + HALF * half + i] = stream[half, :, i].reshape(cols, LANES).astype(BF16)
+            row = stream[half, at, i].reshape(span, LANES)
+            (yp0, yp1)[layer][1 + HALF * half + i, pl.ds(g * span, span)] = row.astype(BF16)
+            if layer == 0:
+                fedn[HALF * half + i, g * span : (g + 1) * span] = row
+
+    def multiply0(g):
+        at = pl.ds(g * span, span)
+        lines = [yp0[r, at] for r in range(rows + 2)]
+        lines[0] = jnp.where(t == 0, jnp.zeros_like(lines[0]), lines[0])
+        lines[-1] = jnp.where(t == tiles - 1, jnp.zeros_like(lines[-1]), lines[-1])
+        lhs = [jnp.concatenate(lines[r : r + 3], axis=1) for r in range(rows)]
+        result = dot(jnp.concatenate(lhs, axis=0), pc[0])
+        for r in range(rows):
+            taps[r, g * span : (g + 1) * span] = result[span * r : span * (r + 1)]
+            if g == 0:
+                taps[r, cols : cols + 8] = result[span * r : span * r + 8]
+                fedn[r, cols : cols + 8] = fedn[r, 0:8]
+
+    def add0(g):
+        start = g * span + HALF
+        at = g * span + lax.broadcasted_iota(jnp.int32, (span, LANES), 0)
+        for r in range(rows):
+            left = taps[r, start - 1 : start - 1 + span, 0:LANES]
+            mid = taps[r, start : start + span, LANES : 2 * LANES]
+            right = taps[r, start + 1 : start + 1 + span, 2 * LANES : 3 * LANES]
+            left = jnp.where(at == cols - HALF, 0.0, left)
+            right = jnp.where(at == cols - HALF - 1, 0.0, right)
+            row = fedn[r, start : start + span] + (left + mid + right + small[4:5, :])
+            stream[r // HALF, pl.ds(g * GROUP, GROUP), r % HALF] = row.reshape(GROUP, WIN, LANES)
 
     def convolve(layer, r, first_col, last_col):
         yp = (yp0, yp1)[layer]
@@ -204,34 +247,11 @@
         fed = stream[r // HALF, :, r % HALF].reshape(cols, LANES)
         return fed + (total + small[4 + layer : 5 + layer, :])
 
-    inner = list(range(1, rows - 1))
-
     def put0(n, mixed):
         mix0[0, n] = mixed[0:32]
         mix0[1, n] = mixed[32:64]
 
-    def step0(g, carry):
-        pair_copy(g).wait_recv()
-        attend(0, kv0, g, put0)
-        return carry
-
-    lax.fori_loop(0, groups, step0, 0)
-    for half in range(2):
-        feed(0, mix0, half)
-        halo_copy(0, half).start()
-
-    def finish0(r):
-        row = pltpu.roll(convolve(0, r, 0, cols - 1), cols - HALF, 0)
-        stream[r // HALF, :, r % HALF] = row.reshape(windows, WIN, LANES)
-
-    for r in inner:
-        finish0(r)
-    for side in range(2):
-        halo_copy(0, side).wait_recv()
-    finish0(0)
-    finish0(rows - 1)
-
-    for g in range(groups):
+    def send_odd(g):
         at = pl.ds(g * GROUP, GROUP)
         for half in range(2):
             x = stream[half, at].reshape(GROUP * 32, LANES)
@@ -243,31 +263,50 @@
         for copy in odd_copies(g):
             copy.start()
 
+    for g in range(groups + 1):
+        if g < groups:
+            pair_copy(g).wait_recv()
+            attend(0, kv0, g, put0)
+            for half in range(2):
+                feed(0, mix0, half, g)
+                halo_copy(0, half, g).start()
+        if g >= 1:
+            for side in range(2):
+                halo_copy(0, side, g - 1).wait_recv()
+            multiply0(g - 1)
+        if g >= 2:
+            add0(g - 2)
+            send_odd(g - 2)
+    add0(groups - 1)
+    send_odd(groups - 1)
+    pad_weights(1)
+
     def put1(n, mixed):
         mix1[1, n] = mixed[0:32]
         ret[n] = mixed[32:64]
 
-    def step1(g, carry):
+    for g in range(groups):
         for copy in odd_copies(g):
             copy.wait_recv()
         attend(1, kv1, g, put1)
         ret_copy(g).start()
-        return carry
-
-    lax.fori_loop(0, groups, step1, 0)
-    feed(1, mix1, 1)
+        feed(1, mix1, 1, g)
+        if g >= 1:
+            ret_copy(g - 1).wait_recv()
+            feed(1, mix1, 0, g - 1)
     halo_copy(1, 1).start()
-    for g in range(groups):
-        ret_copy(g).wait_recv()
-    feed(1, mix1, 0)
-    halo_copy(1, 0).start()
 
     def finish1(r):
         row = convolve(1, r, cols - HALF, cols - HALF - 1)
         row = pltpu.roll(row.T, HALF, 1)
         xs[pl.ds(r, channels, stride=rows), :] = row[0:channels]
 
-    for r in inner:
+    for r in range(HALF + 1, rows - 1):
+        finish1(r)
+    ret_copy(groups - 1).wait_recv()
+    feed(1, mix1, 0, groups - 1)
+    halo_copy(1, 0).start()
+    for r in range(1, HALF + 1):
         finish1(r)
     for side in range(2):
         halo_copy(1, side).wait_recv()
@@ -280,9 +319,10 @@
         for copy in odd_copies(g):
             copy.wait_send()
         ret_copy(g).wait_send()
-    for layer in range(LAYERS):
         for side in range(2):
-            halo_copy(layer, side).wait_send()
+            halo_copy(0, side, g).wait_send()
+    for side in range(2):
+        halo_copy(1, side).wait_send()
 
 
 def on_device(*args):
@@ -295,11 +335,15 @@
     return pl.pallas_call(
         kernel,
         out_shape=jax.ShapeDtypeStruct(frames.shape, BF16),
-        in_specs=[vmem] * len(args),
+        in_specs=[pl.BlockSpec(memory_space=pltpu.HBM)] * len(args),
         out_specs=vmem,
-        scratch_shapes=[
+        scratch_shapes=[pltpu.VMEM(arg.shape, arg.dtype) for arg in args]
+        + [
+            dma((len(args),)),
             pltpu.VMEM((channels * rows, cols), F32),
             pltpu.VMEM((2, windows, HALF, WIN, LANES), F32),
+            pltpu.VMEM((rows, cols + 8, LANES), F32),
+            pltpu.VMEM((rows, cols + 8, 384), F32),
             pltpu.VMEM((windows, 128, LANES), BF16),
             pltpu.VMEM((windows, 128, LANES), BF16),
             pltpu.VMEM((windows, 32, LANES), BF16),
@@ -318,10 +362,10 @@
             dma((groups,)), dma((groups,)),
             dma((3, groups)), dma((3, groups)),
             dma((groups,)), dma((groups,)),
-            dma((LAYERS, 2)), dma((LAYERS, 2)),
+            dma((groups + 1, 2)), dma((groups + 1, 2)),
         ],
         compiler_params=pltpu.CompilerParams(
-            collective_id=0, has_side_effects=True, vmem_limit_bytes=40 * 2**20
+            collective_id=0, has_side_effects=True, vmem_limit_bytes=63 * 2**20
         ),
     )(*args)
 

time: 45.9 us -> 39.2 us (0.85)
  local copies, waits for them, and re-layouts: 8.5 us -> 1.65 us
    unnamed x19 -> x1, local copies, waits for them, and re-layouts: 8.5 us -> 1.65 us
where the time goes in v1:
time: 39.2 us; the launch traced here: 39.1 us
  Pallas kernels  37.4 us (95%)
  local copies, waits for them, and re-layouts  1.65 us (4%)
    pallas_call x1, Pallas kernels, on_device(): pl.pallas_call(kernel, out_shape=jax.ShapeDtypeStruct(frames.shape, BF16)...  37.4 us
    unnamed x1, local copies, waits for them, and re-layouts  1.65 us

profile of v1, /device:TPU:13, one launch (start us, length us, event | category | flops | bytes accessed | tf_op | source)
XLA Modules:
  0.0 39.1 jit_solution(16262709370298438533)
XLA Ops:
  0.0 37.4 %shard_map.91 = bf16[1,120,8,128]{3,2,1,0:T(8,128)(2,1)} custom-call(bf16[1,120,8,128]{3,2,1,0:T(8,128)(2,1)} %frames_h.1, f32[2,2,120]{2,1,0:T(2,128)} %ln_gain_h.1, bf16[2,120,360]{2,1,0:T(8,128)(2,1)} %qkv_h.1, bf16[2,120,120]{2,1,0:T(8,128)(2,1)} %out_h.1, bf16[2,120,240]{2,1,0:T(8,128)(2,1)} %gate_h.1, bf16[2,120,240]{2,1,0:T(8,128)(2,1)} %up_h.1, ...), custom_call_target="tpu_custom_call" | custom-call | tf_op jit(solution)/shard_map/pallas_call | solution.py:335
  37.4 1.7 %copy.11 = bf16[1,120,8,128]{3,2,1,0:T(8,128)(2,1)} copy(bf16[1,120,8,128]{3,2,1,0:T(8,128)(2,1)} %shard_map.91) | data formatting | bytes 491520

commit v2 on v1

--- a/solution.py
+++ b/solution.py
@@ -144,6 +144,7 @@
             part = whole if j == 0 else pltpu.roll(whole, 384 - channels * j, 1)
             part = part[:, 0:LANES]
             part = jnp.where(lanes_of(part.shape) < channels, part, 0.0)
+            part = part if j == 1 else part.T
             pq[layer, :, LANES * j : LANES * (j + 1)] = part.astype(BF16)
         tmp[0:LANES, 0:384] = jnp.zeros((LANES, 384), F32)
         for j, weight in enumerate((gate_w, up_w)):
@@ -167,28 +168,44 @@
     scale = HD ** (-0.5) * 1.4426950408889634
 
     def attend(layer, kv, g, put):
-        at = pl.ds(g * GROUP, GROUP)
-        all_in = kv[at].reshape(GROUP * 128, LANES)
-        q_in = kv[at, pl.ds(0, 64)].reshape(GROUP * 64, LANES)
-        packed = dot(all_in, pq[layer, :, LANES:384]).astype(BF16)
-        queries = dot(q_in, pq[layer, :, 0:LANES]).astype(BF16).astype(F32)
+        all_in = kv[pl.ds(g * GROUP, GROUP)].reshape(GROUP * 128, LANES)
+        keys = dot(all_in, pq[layer, :, LANES : 2 * LANES]).astype(BF16)
+        values = dot_nt(pq[layer, :, 2 * LANES : 3 * LANES], all_in)
+        ones = jnp.ones((LANES - channels, GROUP * 128), F32)
+        values = jnp.concatenate([values[0:channels], ones], axis=0).astype(BF16)
+        twice = [all_in[128 * i : 128 * i + 64] for i in range(GROUP) for _ in range(2)]
+        queries = dot_nt(pq[layer, :, 0:LANES], jnp.concatenate(twice, axis=0))
+        two = 2 * HD
+        keep = (lanes_of((two, LANES)) < 64) == (
+            lax.broadcasted_iota(jnp.int32, (two, LANES), 0) < HD
+        )
         lane = lanes_of((64, LANES))
-        head = [(lane >= HD * h) & (lane < HD * (h + 1)) for h in range(HEADS)]
-        ones = jnp.ones((128, LANES), BF16)
+        first = lane < HD
+        for h in range(2, HEADS, 2):
+            first |= (lane >= HD * h) & (lane < HD * (h + 1))
         for i in range(GROUP):
-            q = queries[64 * i : 64 * (i + 1)]
-            q = jnp.concatenate([jnp.where(head[h], q, 0.0).astype(BF16) for h in range(HEADS)], axis=0)
-            k = packed[128 * i : 128 * (i + 1), 0:LANES]
-            v = jnp.concatenate([packed[128 * i : 128 * (i + 1), LANES:256], ones], axis=1)
-            scores = dot_nt(q, k)
-            top = jnp.max(scores, axis=-1, keepdims=True)
+            at = slice(128 * i, 128 * (i + 1))
+            blocks = []
+            for j in range(HEADS // 2):
+                block = jnp.where(keep, queries[two * j : two * (j + 1), at], 0.0)
+                below_rows = LANES - two * (j + 1)
+                pieces = [jnp.zeros((two * j, LANES), F32)] if j else []
+                pieces += [block, jnp.zeros((below_rows, LANES), F32)]
+                blocks.append(jnp.concatenate(pieces, axis=0))
+            spread = jnp.concatenate(blocks, axis=1).astype(BF16)
+            scores = dot(keys[at], spread)
+            top = jnp.max(scores, axis=0, keepdims=True)
             weights = jnp.exp2((scores - top) * scale).astype(BF16)
-            both = dot(weights, v)
-            mixed, total = both[0:64, 0:LANES], both[0:64, LANES:256]
-            for h in range(1, HEADS):
-                mixed = jnp.where(head[h], both[64 * h : 64 * (h + 1), 0:LANES], mixed)
-                total = jnp.where(head[h], both[64 * h : 64 * (h + 1), LANES:256], total)
-            mixed = (mixed / total).astype(BF16)
+            both = dot(values[:, at], weights)
+            inverse = 1.0 / both[channels:LANES]
+            pieces = []
+            for j in range(HEADS // 2):
+                cut = slice(LANES * j, LANES * (j + 1))
+                for e in range(two * j, two * (j + 1), 8):
+                    pieces.append(both[e : e + 8, cut] * inverse[:, cut])
+            pieces.append(jnp.zeros((LANES - channels, LANES), F32))
+            turned = jnp.concatenate(pieces, axis=0).T
+            mixed = jnp.where(first, turned[0:64], turned[64:128]).astype(BF16)
             put(g * GROUP + i, mixed)
 
     def feed(layer, mix, half, g):

time: 39.2 us -> 41.2 us (1.051)
  Pallas kernels: 37.4 us -> 39.4 us
    pallas_call x1, Pallas kernels: 37.4 us -> 39.4 us  [on_device(): pl.pallas_call(kernel, out_shape=jax.ShapeDtypeStruct(frames.shape, BF16)...]
where the time goes in v2:
time: 41.2 us; the launch traced here: 41 us
  Pallas kernels  39.4 us (96%)
  local copies, waits for them, and re-layouts  1.65 us (4%)
    pallas_call x1, Pallas kernels, on_device(): pl.pallas_call(kernel, out_shape=jax.ShapeDtypeStruct(frames.shape, BF16)...  39.4 us
    unnamed x1, local copies, waits for them, and re-layouts  1.65 us

profile of v2, /device:TPU:13, one launch (start us, length us, event | category | flops | bytes accessed | tf_op | source)
XLA Modules:
  0.0 41.0 jit_solution(10161662875574644433)
XLA Ops:
  0.0 39.4 %shard_map.91 = bf16[1,120,8,128]{3,2,1,0:T(8,128)(2,1)} custom-call(bf16[1,120,8,128]{3,2,1,0:T(8,128)(2,1)} %frames_h.1, f32[2,2,120]{2,1,0:T(2,128)} %ln_gain_h.1, bf16[2,120,360]{2,1,0:T(8,128)(2,1)} %qkv_h.1, bf16[2,120,120]{2,1,0:T(8,128)(2,1)} %out_h.1, bf16[2,120,240]{2,1,0:T(8,128)(2,1)} %gate_h.1, bf16[2,120,240]{2,1,0:T(8,128)(2,1)} %up_h.1, ...), custom_call_target="tpu_custom_call" | custom-call | tf_op jit(solution)/shard_map/pallas_call | solution.py:352
  39.4 1.7 %copy.11 = bf16[1,120,8,128]{3,2,1,0:T(8,128)(2,1)} copy(bf16[1,120,8,128]{3,2,1,0:T(8,128)(2,1)} %shard_map.91) | data formatting | bytes 491520

commit v3 on v1

--- a/solution.py
+++ b/solution.py
@@ -41,7 +41,7 @@
 def kernel(
     frames_h, ln_gain_h, qkv_h, out_h, gate_h, up_h, down_h, conv_h, conv_b_h, out,
     frames, ln_gain, qkv_w, out_w, gate_w, up_w, down_w, conv_w, conv_b, load_sem,
-    xs, stream, fedn, taps, kv0, kv1, bsend, ret, mix0, mix1, yp0, yp1,
+    xs, stream, fedn, taps, final, kv0, kv1, bsend, ret, mix0, mix1, yp0, yp1,
     pq, po, pgu, pd, pc, tmp, small,
     send0, recv0, send1, recv1, send_ret, recv_ret, send_halo, recv_halo,
 ):
@@ -100,10 +100,10 @@
         at = pl.ds(g * GROUP, GROUP)
         return remote(ret.at[at], mix1.at[0, at], send_ret.at[g], recv_ret.at[g], {"tile": below})
 
-    def halo_copy(layer, side, g=0):
+    def halo_copy(layer, side, g):
         yp = (yp0, yp1)[layer]
-        at = pl.ds(g * span, span) if layer == 0 else pl.ds(0, cols)
-        slot = g if layer == 0 else groups
+        at = pl.ds(g * span, span)
+        slot = layer * groups + g
         if side == 0:
             src, dst, peer = yp.at[1, at], yp.at[rows + 1, at], {"tile": above}
         else:
@@ -204,19 +204,23 @@
         for i in range(HALF):
             row = stream[half, at, i].reshape(span, LANES)
             (yp0, yp1)[layer][1 + HALF * half + i, pl.ds(g * span, span)] = row.astype(BF16)
-            if layer == 0:
-                fedn[HALF * half + i, g * span : (g + 1) * span] = row
-
-    def multiply0(g):
+            off = 8 * layer + g * span
+            fedn[HALF * half + i, off : off + span] = row
+
+    def multiply(layer, g):
         at = pl.ds(g * span, span)
-        lines = [yp0[r, at] for r in range(rows + 2)]
+        lines = [(yp0, yp1)[layer][r, at] for r in range(rows + 2)]
         lines[0] = jnp.where(t == 0, jnp.zeros_like(lines[0]), lines[0])
         lines[-1] = jnp.where(t == tiles - 1, jnp.zeros_like(lines[-1]), lines[-1])
         lhs = [jnp.concatenate(lines[r : r + 3], axis=1) for r in range(rows)]
-        result = dot(jnp.concatenate(lhs, axis=0), pc[0])
+        result = dot(jnp.concatenate(lhs, axis=0), pc[layer])
+        off = 8 * layer + g * span
         for r in range(rows):
-            taps[r, g * span : (g + 1) * span] = result[span * r : span * (r + 1)]
-            if g == 0:
+            taps[r, off : off + span] = result[span * r : span * (r + 1)]
+            if layer == 1 and g == groups - 1:
+                taps[r, 0:8] = result[span * (r + 1) - 8 : span * (r + 1)]
+                fedn[r, 0:8] = fedn[r, cols : cols + 8]
+            if layer == 0 and g == 0:
                 taps[r, cols : cols + 8] = result[span * r : span * r + 8]
                 fedn[r, cols : cols + 8] = fedn[r, 0:8]
 
@@ -232,20 +236,19 @@
             row = fedn[r, start : start + span] + (left + mid + right + small[4:5, :])
             stream[r // HALF, pl.ds(g * GROUP, GROUP), r % HALF] = row.reshape(GROUP, WIN, LANES)
 
-    def convolve(layer, r, first_col, last_col):
-        yp = (yp0, yp1)[layer]
-        parts = [yp[r], yp[r + 1], yp[r + 2]]
-        if r == 0:
-            parts[0] = jnp.where(t == 0, jnp.zeros_like(parts[0]), parts[0])
-        if r == rows - 1:
-            parts[2] = jnp.where(t == tiles - 1, jnp.zeros_like(parts[2]), parts[2])
-        taps = dot(jnp.concatenate(parts, axis=1), pc[layer])
-        at = lax.broadcasted_iota(jnp.int32, (cols, LANES), 0)
-        total = taps[:, LANES : 2 * LANES]
-        total += jnp.where(at == first_col, 0.0, pltpu.roll(taps[:, 0:LANES], 1, 0))
-        total += jnp.where(at == last_col, 0.0, pltpu.roll(taps[:, 2 * LANES :], cols - 1, 0))
-        fed = stream[r // HALF, :, r % HALF].reshape(cols, LANES)
-        return fed + (total + small[4 + layer : 5 + layer, :])
+    def add1(g):
+        start = g * span + HALF
+        at = g * span + lax.broadcasted_iota(jnp.int32, (span, LANES), 0)
+        for r in range(rows):
+            left = taps[r, start - 1 : start - 1 + span, 0:LANES]
+            mid = taps[r, start : start + span, LANES : 2 * LANES]
+            right = taps[r, start + 1 : start + 1 + span, 2 * LANES : 3 * LANES]
+            if g == 0:
+                left = jnp.where(at == 0, 0.0, left)
+            if g == groups - 1:
+                right = jnp.where(at == cols - 1, 0.0, right)
+            row = fedn[r, start : start + span] + (left + mid + right + small[5:6, :])
+            final[r, g * span : (g + 1) * span] = row
 
     def put0(n, mixed):
         mix0[0, n] = mixed[0:32]
@@ -267,16 +270,17 @@
         if g < groups:
             pair_copy(g).wait_recv()
             attend(0, kv0, g, put0)
+        if g >= 1:
+            for side in range(2):
+                halo_copy(0, side, g - 1).wait_recv()
+            multiply(0, g - 1)
+        if g >= 2:
+            add0(g - 2)
+            send_odd(g - 2)
+        if g < groups:
             for half in range(2):
                 feed(0, mix0, half, g)
                 halo_copy(0, half, g).start()
-        if g >= 1:
-            for side in range(2):
-                halo_copy(0, side, g - 1).wait_recv()
-            multiply0(g - 1)
-        if g >= 2:
-            add0(g - 2)
-            send_odd(g - 2)
     add0(groups - 1)
     send_odd(groups - 1)
     pad_weights(1)
@@ -285,33 +289,27 @@
         mix1[1, n] = mixed[0:32]
         ret[n] = mixed[32:64]
 
-    for g in range(groups):
-        for copy in odd_copies(g):
-            copy.wait_recv()
-        attend(1, kv1, g, put1)
-        ret_copy(g).start()
-        feed(1, mix1, 1, g)
-        if g >= 1:
+    for g in range(groups + 2):
+        if g < groups:
+            for copy in odd_copies(g):
+                copy.wait_recv()
+            attend(1, kv1, g, put1)
+            ret_copy(g).start()
+            feed(1, mix1, 1, g)
+            halo_copy(1, 1, g).start()
+        if 1 <= g <= groups:
             ret_copy(g - 1).wait_recv()
             feed(1, mix1, 0, g - 1)
-    halo_copy(1, 1).start()
-
-    def finish1(r):
-        row = convolve(1, r, cols - HALF, cols - HALF - 1)
-        row = pltpu.roll(row.T, HALF, 1)
-        xs[pl.ds(r, channels, stride=rows), :] = row[0:channels]
-
-    for r in range(HALF + 1, rows - 1):
-        finish1(r)
-    ret_copy(groups - 1).wait_recv()
-    feed(1, mix1, 0, groups - 1)
-    halo_copy(1, 0).start()
-    for r in range(1, HALF + 1):
-        finish1(r)
-    for side in range(2):
-        halo_copy(1, side).wait_recv()
-    finish1(0)
-    finish1(rows - 1)
+            halo_copy(1, 0, g - 1).start()
+        if g >= 2:
+            for side in range(2):
+                halo_copy(1, side, g - 2).wait_recv()
+            multiply(1, g - 2)
+            if g >= 3:
+                add1(g - 2)
+    add1(0)
+    for r in range(rows):
+        xs[pl.ds(r, channels, stride=rows), :] = final[r].T[0:channels]
     out[0] = xs[...].reshape(channels, rows, cols).astype(BF16)
 
     for g in range(groups):
@@ -321,8 +319,7 @@
         ret_copy(g).wait_send()
         for side in range(2):
             halo_copy(0, side, g).wait_send()
-    for side in range(2):
-        halo_copy(1, side).wait_send()
+            halo_copy(1, side, g).wait_send()
 
 
 def on_device(*args):
@@ -344,6 +341,7 @@
             pltpu.VMEM((2, windows, HALF, WIN, LANES), F32),
             pltpu.VMEM((rows, cols + 8, LANES), F32),
             pltpu.VMEM((rows, cols + 8, 384), F32),
+            pltpu.VMEM((rows, cols, LANES), F32),
             pltpu.VMEM((windows, 128, LANES), BF16),
             pltpu.VMEM((windows, 128, LANES), BF16),
             pltpu.VMEM((windows, 32, LANES), BF16),
@@ -362,7 +360,7 @@
             dma((groups,)), dma((groups,)),
             dma((3, groups)), dma((3, groups)),
             dma((groups,)), dma((groups,)),
-            dma((groups + 1, 2)), dma((groups + 1, 2)),
+            dma((LAYERS * groups, 2)), dma((LAYERS * groups, 2)),
         ],
         compiler_params=pltpu.CompilerParams(
             collective_id=0, has_side_effects=True, vmem_limit_bytes=63 * 2**20

time: 39.2 us -> 40.8 us (1.041)
  Pallas kernels: 37.4 us -> 39 us
    pallas_call x1, Pallas kernels: 37.4 us -> 39 us  [on_device(): pl.pallas_call(kernel, out_shape=jax.ShapeDtypeStruct(frames.shape, BF16)...]
where the time goes in v3:
time: 40.8 us; the launch traced here: 40.7 us
  Pallas kernels  39 us (96%)
  local copies, waits for them, and re-layouts  1.65 us (4%)
    pallas_call x1, Pallas kernels, on_device(): pl.pallas_call(kernel, out_shape=jax.ShapeDtypeStruct(frames.shape, BF16)...  39 us
    unnamed x1, local copies, waits for them, and re-layouts  1.65 us

profile of v3, /device:TPU:13, one launch (start us, length us, event | category | flops | bytes accessed | tf_op | source)
XLA Modules:
  0.0 40.7 jit_solution(2037276107146664660)
XLA Ops:
  0.0 39.0 %shard_map.91 = bf16[1,120,8,128]{3,2,1,0:T(8,128)(2,1)} custom-call(bf16[1,120,8,128]{3,2,1,0:T(8,128)(2,1)} %frames_h.1, f32[2,2,120]{2,1,0:T(2,128)} %ln_gain_h.1, bf16[2,120,360]{2,1,0:T(8,128)(2,1)} %qkv_h.1, bf16[2,120,120]{2,1,0:T(8,128)(2,1)} %out_h.1, bf16[2,120,240]{2,1,0:T(8,128)(2,1)} %gate_h.1, bf16[2,120,240]{2,1,0:T(8,128)(2,1)} %up_h.1, ...), custom_call_target="tpu_custom_call" | custom-call | tf_op jit(solution)/shard_map/pallas_call | solution.py:332
  39.0 1.7 %copy.11 = bf16[1,120,8,128]{3,2,1,0:T(8,128)(2,1)} copy(bf16[1,120,8,128]{3,2,1,0:T(8,128)(2,1)} %shard_map.91) | data formatting | bytes 491520

commit v4 on v1

--- a/solution.py
+++ b/solution.py
@@ -203,7 +203,7 @@
         stream[half, at] = x.reshape(GROUP, HALF, WIN, LANES)
         for i in range(HALF):
             row = stream[half, at, i].reshape(span, LANES)
-            (yp0, yp1)[layer][1 + HALF * half + i, pl.ds(g * span, span)] = row.astype(BF16)
+            (yp0, yp1)[layer][1 + HALF * half + i, pl.ds(pl.multiple_of(g * span, span) if layer else g * span, span)] = row.astype(BF16)
             if layer == 0:
                 fedn[HALF * half + i, g * span : (g + 1) * span] = row
 
@@ -285,15 +285,20 @@
         mix1[1, n] = mixed[0:32]
         ret[n] = mixed[32:64]
 
-    for g in range(groups):
+    def step1(g, carry):
         for copy in odd_copies(g):
             copy.wait_recv()
         attend(1, kv1, g, put1)
         ret_copy(g).start()
         feed(1, mix1, 1, g)
-        if g >= 1:
-            ret_copy(g - 1).wait_recv()
-            feed(1, mix1, 0, g - 1)
+        return carry
+
+    def step2(g, carry):
+        ret_copy(g).wait_recv()
+        feed(1, mix1, 0, g)
+        return carry
+
+    lax.fori_loop(0, groups, step1, 0)
     halo_copy(1, 1).start()
 
     def finish1(r):
@@ -303,8 +308,7 @@
 
     for r in range(HALF + 1, rows - 1):
         finish1(r)
-    ret_copy(groups - 1).wait_recv()
-    feed(1, mix1, 0, groups - 1)
+    lax.fori_loop(0, groups, step2, 0)
     halo_copy(1, 0).start()
     for r in range(1, HALF + 1):
         finish1(r)

time: 39.2 us -> 38.1 us (0.972)
  Pallas kernels: 37.4 us -> 36.2 us
    pallas_call x1, Pallas kernels: 37.4 us -> 36.2 us  [on_device(): pl.pallas_call(kernel, out_shape=jax.ShapeDtypeStruct(frames.shape, BF16)...]
where the time goes in v4:
time: 38.1 us; the launch traced here: 37.9 us
  Pallas kernels  36.2 us (95%)
  local copies, waits for them, and re-layouts  1.65 us (4%)
    pallas_call x1, Pallas kernels, on_device(): pl.pallas_call(kernel, out_shape=jax.ShapeDtypeStruct(frames.shape, BF16)...  36.2 us
    unnamed x1, local copies, waits for them, and re-layouts  1.65 us

profile of v4, /device:TPU:13, one launch (start us, length us, event | category | flops | bytes accessed | tf_op | source)
XLA Modules:
  0.0 37.9 jit_solution(10257703452193824405)
XLA Ops:
  0.0 36.2 %shard_map.91 = bf16[1,120,8,128]{3,2,1,0:T(8,128)(2,1)} custom-call(bf16[1,120,8,128]{3,2,1,0:T(8,128)(2,1)} %frames_h.1, f32[2,2,120]{2,1,0:T(2,128)} %ln_gain_h.1, bf16[2,120,360]{2,1,0:T(8,128)(2,1)} %qkv_h.1, bf16[2,120,120]{2,1,0:T(8,128)(2,1)} %out_h.1, bf16[2,120,240]{2,1,0:T(8,128)(2,1)} %gate_h.1, bf16[2,120,240]{2,1,0:T(8,128)(2,1)} %up_h.1, ...), custom_call_target="tpu_custom_call" | custom-call | tf_op jit(solution)/shard_map/pallas_call | solution.py:339
  36.3 1.7 %copy.11 = bf16[1,120,8,128]{3,2,1,0:T(8,128)(2,1)} copy(bf16[1,120,8,128]{3,2,1,0:T(8,128)(2,1)} %shard_map.91) | data formatting | bytes 491520
